TPU v7x, 768 devices: a whole 4x8x12 slice. The times are simulated.
768 devices in a mesh: section: 16 (over y_hi, x, core), shard: 12 (over z), replica: 4 (over y_lo).
Axes of the slice: x: 4, y: 8 (y_hi: 2, y_lo: 4; y = y_hi * 4 + y_lo), z: 12, core: 2. Of those that a mesh axis runs over, the one named last changes fastest.
Arguments:
- normed: bfloat16 [16, 2, 6144, 4096], P('section', None, ('shard', 'replica')), may hold values from -0.0546875 to 0.0546875
- key_cotangent: bfloat16 [16, 2, 6144, 512], P('section', None, ('shard', 'replica')), may hold values from -12 to 12
- positions: int32 [2, 6144], P(None, ('shard', 'replica')), may hold values from 0 to 1023, as said below
- key_weight: bfloat16 [16, 4128, 512], P('section', 'shard'), may hold values from -0.09375 to 0.09375
Outputs:
- key_weight_grad: bfloat16 [16, 4128, 512], P('section', 'shard')
- passed_grad: bfloat16 [16, 2, 6144, 4096], P('section', None, ('shard', 'replica'))
Inputs may be any that keep to these rules, and one draw needn't show every extreme that they name: `positions`: each token's position within its document of the micro-batch; in every micro-batch a document begins at every multiple of 1024 tokens, and in all but the first micro-batch at further places drawn at random.
All inputs are finite; a program needn't handle non-finite values.
Results may differ from a plain program's by a relative error of at most 0.018.
Values may be sent and summed in bfloat16 or wider, within the bound.
A program may use at most 64 MiB of HBM per device.

v0:
```python
import jax
import jax.numpy as jnp
from jax import lax
from jax.sharding import PartitionSpec as P

HEAD = 128


def shifted(value, axis, steps):
    count = lax.axis_size(axis)
    leading, last = (max(0, -steps), min(count, count - steps))
    return lax.ppermute(value, axis, [(source, source + steps) for source in range(leading, last)])


def undo_rotation(cotangent, positions):
    half = HEAD // 2
    heads = cotangent.shape[-1] // HEAD
    index = jnp.arange(half, dtype=jnp.float32)
    freq = jnp.power(jnp.float32(500000.0), -2.0 * index / HEAD)
    angle = positions.astype(jnp.float32)[..., None] * freq
    angle = jnp.concatenate([angle, angle], axis=-1)[:, :, None, :]
    cosine = jnp.cos(angle)
    sine = jnp.sin(angle)
    lead = cotangent.shape[:2]
    grads = cotangent.astype(jnp.float32).reshape(lead + (heads, HEAD))
    swapped = jnp.concatenate([grads[..., half:], -grads[..., :half]], axis=-1)
    result = grads * cosine + swapped * sine
    return result.reshape(lead + (heads * HEAD,)).astype(jnp.bfloat16)


def per_device(normed, key_cotangent, positions, key_weight):
    key_grad = undo_rotation(key_cotangent[0], positions)
    width = normed.shape[3]
    local_rows = key_weight[0]
    moved = jnp.einsum(
        "mtk,dk->mtd",
        key_grad,
        lax.all_gather(local_rows, "shard", axis=0, tiled=True),
        preferred_element_type=jnp.float32,
    ).astype(jnp.bfloat16)
    input_grad = moved[:, :, :width][None]
    passed = shifted(input_grad, "section", -1)
    steps_tok = normed.shape[1] * normed.shape[2]
    flat_in = normed[0].reshape(steps_tok, width)
    flat_key = key_grad.reshape(steps_tok, key_grad.shape[-1])
    padding = lax.axis_size("shard") * local_rows.shape[0] - width
    padded = jnp.pad(flat_in, ((0, 0), (0, padding)))
    shard_total = lax.psum_scatter(
        lax.dot_general(
            padded, flat_key, (((0,), (0,)), ((), ())), preferred_element_type=jnp.float32
        ).astype(jnp.bfloat16),
        "shard",
        scatter_dimension=0,
        tiled=True,
    )
    shard_round = lax.optimization_barrier(shard_total).astype(jnp.float32)
    total = lax.psum(shard_round.astype(jnp.bfloat16), "replica")
    return (total[None], passed)


def solution(mesh):
    in_specs = (
        P("section", None, ("shard", "replica"), None),
        P("section", None, ("shard", "replica"), None),
        P(None, ("shard", "replica")),
        P("section", "shard", None),
    )
    out_specs = (P("section", "shard", None), P("section", None, ("shard", "replica"), None))
    return jax.shard_map(
        per_device, mesh=mesh, in_specs=in_specs, out_specs=out_specs, check_vma=False
    )
```

profile of v0, /device:TPU:1, one launch (start us, length us, event | category | flops | bytes accessed | tf_op | source)
XLA Modules:
  0.0 224.0 jit_solution(14771256792994938770)
XLA Ops:
  7.2 0.0 all-gather.3.cloned.1.call-start
  7.2 0.7 all-gather.3.cloned.1.call-update
  7.9 0.0 reduce-scatter.2.cloned.1.call-start
  7.9 0.7 convert_element_type.40
  8.6 1.1 reshape.55
  9.8 0.1 broadcast_multiply_fusion
  9.9 0.5 fusion.10
  10.4 0.0 copy-start
  10.4 0.4 fusion.12
  10.8 0.0 copy-start.1
  10.8 0.4 maximum_multiply_fusion
  11.2 0.1 mul.56
  11.3 0.1 copy-done
  11.4 0.1 fusion.4
  11.5 0.9 copy-done.1
  12.4 3.3 %convolution_convert_fusion = bf16[4128,512]{1,0:T(8,128)(2,1)} fusion(bf16[256,512]{1,0:T(8,128)(2,1)S(1)} %fusion.4, bf16[256,4096]{1,0:T(8,128)(2,1)S(1)} %bitcast.34), kind=kOutput, calls=%fused_computation | convolution fusion | flops 1084243968 | bytes 6586368 | tf_op jit(solution)/shard_map/dot_general | solution.py:49
  15.7 0.0 reduce-scatter.2.cloned.1.call-update
  15.7 0.0 all-reduce.3.cloned.1.call-start
  15.8 0.2 mul.62
  16.0 0.2 mul.64
  16.2 65.2 %all-gather.3.cloned.1.call-done = bf16[1,4128,512]{2,1,0:T(8,128)(2,1)} async-done(((bf16[1,344,512]{2,1,0:T(8,128)(2,1)}), bf16[1,4128,512]{2,1,0:T(8,128)(2,1)}) %all-gather.3.cloned.1.call-update) | async-done | bytes 4227088 | tf_op jit(solution)/shard_map/all_gather | solution.py:38
  81.4 3.6 %fusion = bf16[2,128,4128]{2,1,0:T(8,128)(2,1)S(1)} fusion(bf16[1,4128,512]{2,1,0:T(8,128)(2,1)} %all-gather.3.cloned.1.call-done, f32[2,128,512]{2,1,0:T(8,128)S(1)} %mul.64, f32[2,128,512]{2,1,0:T(8,128)S(1)} %mul.62, bf16[1,2,128,512]{3,2,1,0:T(8,128)(2,1)S(1)} %copy-done), kind=kOutput, calls=%fused_computation.1 | convolution fusion | flops 1082654720 | bytes 7651328 | tf_op jit(solution)/shard_map/mtk,dk->mtd/dot_general | solution.py:35
  85.0 1.6 fusion.3
  86.5 6.7 %collective-permute-start = (bf16[1,2,128,4096]{3,2,1,0:T(8,128)(2,1)}, bf16[1,2,128,4096]{3,2,1,0:T(8,128)(2,1)S(1)}, u32[]{:S(2)}, u32[]{:S(2)}) collective-permute-start(bf16[1,2,128,4096]{3,2,1,0:T(8,128)(2,1)} %fusion.3), channel_id=1, source_target_pairs={{48,0},{96,48},{144,96},{192,144},{240,192},{288,240},{336,288},{3... | collective-permute-start | bytes 6291464 | tf_op jit(solution)/shard_map/ppermute | solution.py:12
  93.3 54.8 %reduce-scatter.2.cloned.1.call-done = bf16[344,512]{1,0:T(8,128)(2,1)} async-done(((bf16[4128,512]{1,0:T(8,128)(2,1)}), bf16[344,512]{1,0:T(8,128)(2,1)}) %reduce-scatter.2.cloned.1.call-update) | async-done | bytes 352272 | tf_op jit(solution)/shard_map/reduce_scatter | solution.py:48
  148.1 0.0 all-reduce.3.cloned.1.call-update
  148.1 0.0 collective-permute-done
  148.1 66.4 %all-reduce.3.cloned.1.call-done = bf16[1,344,512]{2,1,0:T(8,128)(2,1)} async-done(((bf16[1,344,512]{2,1,0:T(8,128)(2,1)}), bf16[1,344,512]{2,1,0:T(8,128)(2,1)}) %all-reduce.3.cloned.1.call-update) | async-done | bytes 352272 | tf_op jit(solution)/shard_map/psum | solution.py:57
  214.5 1.7 copy.12
  216.2 1.3 copy.13
  (1 shorter events, 0.0 us)
Async XLA Ops:
  7.2 74.2 %all-gather.3.cloned.1.call-start = ((), (), s32[]{:S(2)}) async-start(), calls=%async_computation.3 | async-start | bytes 4579328 | tf_op jit(solution)/shard_map/all_gather | solution.py:38
  7.9 140.2 %reduce-scatter.2.cloned.1.call-start = ((), (), s32[]{:S(2)}) async-start(), calls=%async_computation.1 | async-start | bytes 4579328 | tf_op jit(solution)/shard_map/reduce_scatter | solution.py:48
  10.4 1.0 copy-start
  10.8 1.6 copy-start.1
  15.7 198.7 %all-reduce.3.cloned.1.call-start = ((), (), s32[]{:S(2)}) async-start(), calls=%async_computation.2 | async-start | bytes 704512 | tf_op jit(solution)/shard_map/psum | solution.py:57
  86.5 61.5 %collective-permute-start = (bf16[1,2,128,4096]{3,2,1,0:T(8,128)(2,1)}, bf16[1,2,128,4096]{3,2,1,0:T(8,128)(2,1)S(1)}, u32[]{:S(2)}, u32[]{:S(2)}) collective-permute-start(bf16[1,2,128,4096]{3,2,1,0:T(8,128)(2,1)} %fusion.3), channel_id=1, source_target_pairs={{48,0},{96,48},{144,96},{192,144},{240,192},{288,240},{336,288},{3... | collective-permute-start | bytes 6291464 | tf_op jit(solution)/shard_map/ppermute | solution.py:12
Sparse Core Ops, SparseCore 0:
  10.4 70.9 all-gather.2
  84.5 63.4 reduce-scatter.1
  151.3 63.1 all-reduce.2
where the time goes:
time: 226 us; the launch traced here: 224 us
  waiting for transfers between devices  187 us (83%)
  between operations  13.8 us (6%)
  local copies, waits for them, and re-layouts  7.28 us (3%)
  starting transfers between devices  6.86 us (3%)
  matrix products  6.83 us (3%)
    psum x1, waiting for transfers between devices, per_device(): total = lax.psum(shard_round.astype(jnp.bfloat16), 'replica')  66.4 us
    all_gather x1, waiting for transfers between devices, per_device(): lax.all_gather(local_rows, 'shard', axis=0, tiled=True)  65.2 us
    reduce_scatter x1, waiting for transfers between devices, per_device(): lax.psum_scatter(lax.dot_general(padded, flat_key, (((0,), (0,)), ((), ()...  54.8 us
    ppermute x1, starting transfers between devices, shifted(): lax.ppermute(value, axis, [(source, source + steps) for source in range(l...  6.74 us
  transfers between devices with their start and end apart: 4, of which 3 were waited for; matrix products, arithmetic and copies ran while one was open for 5% of the time, Pallas kernels for 0%

commit v1 on v0

v1 whole, which is shorter than its diff:
```python
import functools

import jax
import jax.numpy as jnp
import numpy as np
from jax import lax
from jax.experimental import pallas as pl
from jax.experimental.pallas import tpu as pltpu
from jax.sharding import PartitionSpec as P

HEAD = 128
RING = 12
ROWS = 344
PAD = 352
KW = 512
TOK = 256
WIDTH = 4096
LAST = 15
CHUNKS = ((0, 96), (96, 96), (192, 80), (272, 80))
NC = len(CHUNKS)
MESH = pl.DeviceIdType.MESH
SUM_EVEN, SUM_ODD = (6, 4, -4, 2, -2, 0), (5, -5, 3, -3, 1, -1)
GET_EVEN, GET_ODD = (0, -2, 2, -4, 4, -6), (-1, 1, -3, 3, -5, 5)
F32, BF16 = jnp.float32, jnp.bfloat16


def kernel(
    normed_hbm, cot_ref, pos_ref, freq_ref, w_ref,
    grad_ref, out_ref,
    normed, flat, send_n, got_n, key, key_next, wsrc, weights, terms, sums,
    cols, send_c, got_c, part, part_in, total_in,
    local_sem, w_sem, k_sem, n_sem, g_sem, r_sem, c_sem, x_sem, t_sem,
):
    s, z, r = (lax.axis_index(a) for a in ("section", "shard", "replica"))
    parity = lax.rem(r, 2)
    odd = lax.rem(z + parity, 2)
    even = odd == 0
    is_odd = odd == 1
    sign = 1 - 2 * lax.rem(s, 2)
    mate = (s, z, r + 1 - 2 * parity)
    across = (s, z, lax.rem(r + 2, 4))
    ahead = (s, lax.rem(z + sign + RING, RING), r)
    behind = (s, lax.rem(z - sign + RING, RING), r)
    before = (jnp.maximum(s - 1, 0), z, r)
    after = (jnp.minimum(s + 1, LAST), z, r)
    to = (ahead, behind)

    def owner(pair, which):
        step = jnp.where(which == 0, pair[0], pair[1])
        return lax.rem(z + sign * step + 2 * RING, RING)

    pending = []

    def push(src, dst, sems, index, device, when=None):
        copy = pltpu.make_async_remote_copy(
            src, dst, sems.at[(0,) + index[0]], sems.at[(1,) + index[1]],
            device_id=device, device_id_type=MESH,
        )
        if when is None:
            copy.start()
        else:
            pl.when(when)(copy.start)
        pending.append((when, copy))

    def arrived(dst, sems, index):
        pltpu.make_async_remote_copy(
            dst, dst, sems.at[(0,) + index], sems.at[(1,) + index],
            device_id=mate, device_id_type=MESH,
        ).wait_recv()

    fetch = pltpu.make_async_copy(normed_hbm, normed, local_sem)
    fetch.start()
    barrier = pltpu.get_barrier_semaphore()
    for device in (mate, across, ahead, behind):
        pl.semaphore_signal(barrier, inc=1, device_id=device, device_id_type=MESH)

    @pl.when(s > 0)
    def _():
        pl.semaphore_signal(barrier, inc=1, device_id=before, device_id_type=MESH)

    @pl.when(s < LAST)
    def _():
        pl.semaphore_signal(barrier, inc=1, device_id=after, device_id_type=MESH)

    wsrc[...] = jnp.concatenate(
        [w_ref[...].astype(F32), jnp.zeros((PAD - ROWS, KW), F32)], axis=0
    ).astype(BF16)

    half = lax.broadcasted_iota(jnp.int32, (TOK // 2, HEAD), 1) < HEAD // 2
    for m in range(2):
        place = jnp.broadcast_to(pos_ref[m : m + 1, :].astype(F32), (HEAD, HEAD)).T
        angle = place * freq_ref[...]
        cosine = jnp.cos(angle)
        sine = jnp.sin(angle)
        sine = jnp.where(half, sine, -sine)
        rows = pl.ds(m * (TOK // 2), TOK // 2)
        for h in range(KW // HEAD):
            lanes = pl.ds(h * HEAD, HEAD)
            g = cot_ref[rows, lanes].astype(F32)
            key[0, rows, lanes] = (
                g * cosine + pltpu.roll(g, HEAD // 2, 1) * sine
            ).astype(BF16)

    pl.semaphore_wait(
        barrier, 4 + (s > 0).astype(jnp.int32) + (s < LAST).astype(jnp.int32)
    )

    mine = lax.div(z, 2)
    for c, (at, size) in enumerate(CHUNKS):
        rows = pl.ds(at, size)
        push(wsrc.at[rows], weights.at[mine, rows], w_sem, ((c,), (c,)), before,
             jnp.logical_and(s > 0, even))
    push(key.at[0], key.at[1], k_sem, ((0,), (0,)), mate)
    push(key.at[0], key_next.at[0], k_sem, ((1,), (1,)), before, s > 0)

    @pl.when(s == LAST)
    def _():
        key_next[...] = jnp.zeros_like(key_next)

        @pl.when(even)
        def _():
            weights[mine] = wsrc[...]

    fetch.wait()
    for i in range(WIDTH // 512):
        flat[pl.ds(512 * i, 512), :] = normed[:, pl.ds(512 * i, 512)].astype(F32).T
    flat[pl.ds(WIDTH, 40), :] = jnp.zeros((40, TOK), F32)

    def block(o):
        return flat[pl.ds(pl.multiple_of(ROWS * o, 8), PAD), :].astype(BF16)

    for n in range(6):
        send_n[n] = block(owner((SUM_ODD[n], SUM_EVEN[n]), odd))
        push(send_n.at[n], got_n.at[n], n_sem, ((n,), (n,)), mate)

    for c, (at, size) in enumerate(CHUNKS):
        rows = pl.ds(at, size)

        @pl.when(jnp.logical_and(s < LAST, even))
        def _():
            arrived(weights.at[mine, rows], w_sem, (c,))

        for d in range(2):
            push(weights.at[mine, rows], weights.at[mine, rows], g_sem,
                 ((d, 0, c), (d, 0, c)), to[d], even)

    arrived(key.at[1], k_sem, (0,))
    push(key.at[1], key_next.at[1], k_sem, ((2,), (2,)), before, s > 0)

    def term(n):
        arrived(got_n.at[n], n_sem, (n,))
        own = block(owner((SUM_EVEN[n], SUM_ODD[n]), odd))
        terms[n] = (
            jnp.dot(own, key[0], preferred_element_type=F32)
            + jnp.dot(got_n[n], key[1], preferred_element_type=F32)
        ).astype(BF16)

    def gather_step(j):
        for c, (at, size) in enumerate(CHUNKS):
            rows = pl.ds(at, size)
            for d in range(2):
                away = 2 * j + 2 - odd
                from_ = lax.rem(z + (2 * d - 1) * sign * away + 2 * RING, RING)
                spot = weights.at[lax.div(from_, 2), rows]
                if j == 2 and d == 1:
                    pl.when(is_odd)(lambda: arrived(spot, g_sem, (d, j, c)))
                    continue
                arrived(spot, g_sem, (d, j, c))
                slot = j + 1 - odd
                if j < 2:
                    push(spot, spot, g_sem, ((d, slot, c), (d, slot, c)), to[d])
                else:
                    push(spot, spot, g_sem, ((d, 2, c), (d, 2, c)), to[d], is_odd)

    def column(n):
        o = owner((GET_EVEN[n], GET_ODD[n]), odd)
        both = lax.dot_general(
            weights[lax.div(o, 2)], key_next[...].reshape(2 * TOK, KW),
            (((1,), (1,)), ((), ())), preferred_element_type=F32,
        )
        cols[pl.ds(pl.multiple_of(ROWS * o, 8), ROWS), :] = both[:ROWS, :TOK]
        send_c[n] = both[:, TOK:].astype(BF16)
        push(send_c.at[n], got_c.at[n], c_sem, ((n,), (n,)), mate)

    def sum_start():
        for c, (at, size) in enumerate(CHUNKS):
            rows = pl.ds(at, size)
            push(terms.at[0, rows], sums.at[0, 0, rows], r_sem, ((0, 0, c), (0, 0, c)),
                 to[0], even)

    def sum_step(j):
        for c, (at, size) in enumerate(CHUNKS):
            rows = pl.ds(at, size)
            for d in range(2):
                n = 2 * j + d + 1 - odd
                slot = j + 1 - odd
                spot = sums.at[d, j, rows]
                there = sums.at[d, slot, rows]

                def add():
                    arrived(spot, r_sem, (d, j, c))
                    spot[...] = (
                        spot[...].astype(F32) + terms[n, rows].astype(F32)
                    ).astype(BF16)

                if (d, j) == (1, 0):
                    pl.when(even)(add)
                    push(spot, there, r_sem, ((d, 1, c), (d, 1, c)), to[d], even)
                    push(terms.at[n, rows], there, r_sem, ((d, 0, c), (d, 0, c)), to[d],
                         is_odd)
                elif j < 2:
                    add()
                    push(spot, there, r_sem, ((d, slot, c), (d, slot, c)), to[d])
                else:
                    pl.when(is_odd)(add)
                    push(spot, sums.at[d, 2, rows], r_sem, ((d, 2, c), (d, 2, c)), to[d],
                         is_odd)
            if j == 2:

                @pl.when(even)
                def _():
                    for d in range(2):
                        arrived(sums.at[d, 2, rows], r_sem, (d, 2, c))
                    part[rows] = (
                        terms[5, rows].astype(F32)
                        + sums[0, 2, rows].astype(F32)
                        + sums[1, 2, rows].astype(F32)
                    ).astype(BF16)

                push(part.at[rows], part_in.at[rows], x_sem, ((c,), (c,)), across, even)

    gather_step(0)

    @pl.when(s < LAST)
    def _():
        arrived(key_next.at[0], k_sem, (1,))
        arrived(key_next.at[1], k_sem, (2,))

    column(0)
    column(1)
    gather_step(1)
    term(0)
    sum_start()
    column(2)
    column(3)
    gather_step(2)
    column(4)
    column(5)
    term(1)
    term(2)
    sum_step(0)
    term(3)
    term(4)
    sum_step(1)
    term(5)
    sum_step(2)

    for n in range(6):
        arrived(got_c.at[n], c_sem, (n,))
        o = owner((GET_ODD[n], GET_EVEN[n]), odd)
        cols[pl.ds(pl.multiple_of(ROWS * o, 8), ROWS), :] = got_c[n].astype(F32)[:ROWS]

    for c, (at, size) in enumerate(CHUNKS):
        rows = pl.ds(at, size)

        @pl.when(even)
        def _():
            arrived(part_in.at[rows], x_sem, (c,))
            total_in[rows] = (
                part[rows].astype(F32) + part_in[rows].astype(F32)
            ).astype(BF16)

        push(total_in.at[rows], total_in.at[rows], t_sem, ((c,), (c,)), mate, even)

    for i in range(WIDTH // 512):
        out_ref[:, pl.ds(512 * i, 512)] = cols[pl.ds(512 * i, 512), :].T.astype(BF16)

    for c, (at, size) in enumerate(CHUNKS):
        rows = pl.ds(at, size)
        pl.when(is_odd)(lambda: arrived(total_in.at[rows], t_sem, (c,)))
    grad_ref[...] = total_in[...].astype(F32)[:ROWS].astype(BF16)

    for when, copy in pending:
        if when is None:
            copy.wait_send()
        else:
            pl.when(when)(copy.wait_send)


def per_device(normed, key_cotangent, positions, key_weight):
    index = np.arange(HEAD) % (HEAD // 2)
    freq = jnp.asarray(np.power(500000.0, -2.0 * index / HEAD)[None], F32)
    vmem = pl.BlockSpec(memory_space=pltpu.VMEM)
    dma = pltpu.SemaphoreType.DMA
    grad, passed = pl.pallas_call(
        kernel,
        out_shape=(
            jax.ShapeDtypeStruct((ROWS, KW), BF16),
            jax.ShapeDtypeStruct((TOK, WIDTH), BF16),
        ),
        in_specs=[pl.BlockSpec(memory_space=pl.ANY)] + [vmem] * 4,
        out_specs=(vmem, vmem),
        scratch_shapes=[
            pltpu.VMEM((TOK, WIDTH), BF16),
            pltpu.VMEM((RING * ROWS + 8, TOK), F32),
            pltpu.VMEM((6, PAD, TOK), BF16),
            pltpu.VMEM((6, PAD, TOK), BF16),
            pltpu.VMEM((2, TOK, KW), BF16),
            pltpu.VMEM((2, TOK, KW), BF16),
            pltpu.VMEM((PAD, KW), BF16),
            pltpu.VMEM((6, PAD, KW), BF16),
            pltpu.VMEM((6, PAD, KW), BF16),
            pltpu.VMEM((2, 3, PAD, KW), BF16),
            pltpu.VMEM((RING * ROWS, TOK), F32),
            pltpu.VMEM((6, PAD, TOK), BF16),
            pltpu.VMEM((6, PAD, TOK), BF16),
            pltpu.VMEM((PAD, KW), BF16),
            pltpu.VMEM((PAD, KW), BF16),
            pltpu.VMEM((PAD, KW), BF16),
            dma,
            dma((2, NC)),
            dma((2, 3)),
            dma((2, 6)),
            dma((2, 2, 3, NC)),
            dma((2, 2, 3, NC)),
            dma((2, 6)),
            dma((2, NC)),
            dma((2, NC)),
        ],
        compiler_params=pltpu.CompilerParams(
            collective_id=0, has_side_effects=True, vmem_limit_bytes=52 << 20
        ),
        cost_estimate=pl.CostEstimate(
            flops=4 * TOK * KW * WIDTH, bytes_accessed=6 << 20, transcendentals=2 * TOK * HEAD
        ),
    )(
        normed.reshape(TOK, WIDTH),
        key_cotangent.reshape(TOK, KW),
        positions,
        freq,
        key_weight.reshape(ROWS, KW),
    )
    return grad[None], passed.reshape(normed.shape)


def solution(mesh):
    in_specs = (
        P("section", None, ("shard", "replica"), None),
        P("section", None, ("shard", "replica"), None),
        P(None, ("shard", "replica")),
        P("section", "shard", None),
    )
    out_specs = (P("section", "shard", None), P("section", None, ("shard", "replica"), None))
    return jax.shard_map(
        per_device, mesh=mesh, in_specs=in_specs, out_specs=out_specs, check_vma=False
    )
```

time: 226 us -> 120 us (0.53)
  the two profiles are of different devices: /device:TPU:1 before, /device:TPU:71 now
where the time goes in v1:
time: 120 us
  Pallas kernels  112 us (93%)
  local copies, waits for them, and re-layouts  7.12 us (6%)
    pallas_call x1, Pallas kernels, per_device(): pl.pallas_call(kernel, out_shape=(jax.ShapeDtypeStruct((ROWS, KW), BF16),...  112 us
    unnamed x10, local copies, waits for them, and re-layouts  7.12 us

profile of v1, /device:TPU:71, one launch (start us, length us, event | category | flops | bytes accessed | tf_op | source)
XLA Modules:
  0.0 120.2 jit_solution(14745194490476000416)
XLA Ops:
  0.6 0.0 copy-start
  0.6 1.0 copy-done
  1.6 0.0 copy-start.1
  1.6 0.9 copy-done.1
  2.6 0.0 copy-start.2
  2.6 0.7 copy-done.2
  3.2 0.0 copy-start.3
  3.2 0.7 copy-done.3
  3.9 112.4 %shard_map.68 = (bf16[344,512]{1,0:T(8,128)(2,1)S(1)}, bf16[256,4096]{1,0:T(8,128)(2,1)}) custom-call(bf16[256,4096]{1,0:T(8,128)(2,1)} %bitcast.9, bf16[256,512]{1,0:T(8,128)(2,1)S(1)} %bitcast.7, s32[2,128]{1,0:T(2,128)S(1)} %copy-done.2, f32[1,128]{1,0:T(1,128)S(1)} %copy-done.3, bf16[344,512]{1,0:T(8,128)(2,1)S(1)} %bitcast.6), custom_call_target="tpu_custom_call" | custom-call | flops 2147483648 | bytes 6291456 | tf_op jit(solution)/shard_map/pallas_call | solution.py:295
  116.3 0.7 copy.9
  117.1 3.1 %copy.10 = bf16[1,2,128,4096]{3,2,1,0:T(8,128)(2,1)} copy(bf16[1,2,128,4096]{3,2,1,0:T(8,128)(2,1)} %bitcast.8) | data formatting | bytes 4194304
Async XLA Ops:
  0.6 1.0 copy-start
  1.6 0.9 copy-start.1
  2.6 0.7 copy-start.2
  3.2 0.7 copy-start.3

commit v2 on v1

v2 whole, which is shorter than its diff:
```python
import functools

import jax
import jax.numpy as jnp
import numpy as np
from jax import lax
from jax.experimental import pallas as pl
from jax.experimental.pallas import tpu as pltpu
from jax.sharding import PartitionSpec as P

HEAD = 128
RING = 12
ROWS = 344
PAD = 352
KW = 512
TOK = 256
WIDTH = 4096
LAST = 15
FAR = 8
CHUNKS = ((0, 96), (96, 96), (192, 80), (272, 80))
NC = len(CHUNKS)
MESH = pl.DeviceIdType.MESH
SUM_EVEN, SUM_ODD = (6, 4, -4, 2, -2, 0), (5, -5, 3, -3, 1, -1)
GET_EVEN, GET_ODD = (0, -2, 2, -4, 4, -6), (-1, 1, -3, 3, -5, 5)
F32, BF16 = jnp.float32, jnp.bfloat16


def kernel(
    normed_hbm, cot_hbm, pos_hbm, w_hbm,
    grad_ref, out_ref,
    normed, cot_ref, pos_ref, w_ref, flat, send_n, got_n, key, key_next, wsrc, weights, terms, sums,
    cols, send_c, got_c, part, part_in, total_in,
    local_sem, w_sem, k_sem, n_sem, g_sem, r_sem, c_sem, p_sem, x_sem, t_sem,
):
    s, z, r = (lax.axis_index(a) for a in ("section", "shard", "replica"))
    inner = jnp.logical_or(r == 1, r == 2)
    outer = jnp.logical_not(inner)
    odd = lax.rem(z + inner.astype(jnp.int32), 2)
    even = odd == 0
    is_odd = odd == 1
    sign = 1 - 2 * lax.rem(s, 2)
    mate_at = r + 1 - 2 * lax.rem(r, 2)
    mate = (s, z, mate_at)
    across = (s, z, 3 - r)
    ahead = (s, lax.rem(z + sign + RING, RING), r)
    behind = (s, lax.rem(z - sign + RING, RING), r)
    lower, upper = jnp.maximum(s - 1, 0), jnp.minimum(s + 1, LAST)
    far_out, far_in = s == FAR, s == FAR - 1
    near_out = jnp.logical_and(s > 0, s != FAR)
    before = (lower, z, r)
    after = (upper, z, r)
    far_before = (lower, z, mate_at)
    far_after = (upper, z, mate_at)
    side = lax.rem(z, 2)
    far_to = (lower, z, jnp.where(r == 3, side, 3 - side))
    far_from = (upper, z, jnp.where(r < 2, 3, 0))
    far_w_out = jnp.logical_and(far_out, outer)
    far_w_in = jnp.logical_and(far_in, even)
    to = (ahead, behind)

    def owner(pair, which):
        step = jnp.where(which == 0, pair[0], pair[1])
        return lax.rem(z + sign * step + 2 * RING, RING)

    pending, chunked = [], []

    def push(src, dst, sems, index, device, when=None):
        copy = pltpu.make_async_remote_copy(
            src, dst, sems.at[(0,) + index[0]], sems.at[(1,) + index[1]],
            device_id=device, device_id_type=MESH,
        )
        if when is None:
            copy.start()
        else:
            pl.when(when)(copy.start)
        pending.append((when, copy))

    def rows(c):
        return pl.ds(*CHUNKS[c])

    def chunks(body):
        for c in range(NC):
            body(c)

    def line(src, dst, sems, index, device, when=None):
        def copy(c):
            return pltpu.make_async_remote_copy(
                src.at[rows(c)], dst.at[rows(c)],
                sems.at[(0,) + index[0] + (c,)], sems.at[(1,) + index[1] + (c,)],
                device_id=device, device_id_type=MESH,
            )

        def run(act):
            if when is None:
                act()
            else:
                pl.when(when)(act)

        chunked.append(lambda c: run(lambda: copy(c).wait_send()))
        return lambda c: run(lambda: copy(c).start())

    def arrived(dst, sems, index):
        pltpu.make_async_remote_copy(
            dst, dst, sems.at[(0,) + index], sems.at[(1,) + index],
            device_id=mate, device_id_type=MESH,
        ).wait_recv()

    fetch = [
        pltpu.make_async_copy(src, dst, local_sem.at[i])
        for i, (src, dst) in enumerate(
            ((w_hbm, w_ref), (normed_hbm, normed), (cot_hbm, cot_ref), (pos_hbm, pos_ref))
        )
    ]
    for copy in fetch:
        copy.start()
    barrier = pltpu.get_barrier_semaphore()
    count = jnp.int32(3)
    for when, device in (
        (None, mate), (None, ahead), (None, behind), (inner, across),
        (s > 0, before), (s < LAST, after), (far_out, far_before), (far_in, far_after),
        (far_w_out, far_to), (far_w_in, far_from),
    ):
        def greet():
            pl.semaphore_signal(barrier, inc=1, device_id=device, device_id_type=MESH)

        if when is None:
            greet()
        else:
            pl.when(when)(greet)
            count = count + when.astype(jnp.int32)

    fetch[0].wait()
    wsrc[...] = jnp.concatenate(
        [w_ref[...].astype(F32), jnp.zeros((PAD - ROWS, KW), F32)], axis=0
    ).astype(BF16)

    fetch[1].wait()
    for i in range(WIDTH // 512):
        flat[pl.ds(512 * i, 512), :] = normed[:, pl.ds(512 * i, 512)].astype(F32).T
    flat[pl.ds(WIDTH, 40), :] = jnp.zeros((40, TOK), F32)

    def block(o):
        return flat[pl.ds(pl.multiple_of(ROWS * o, 8), PAD), :].astype(BF16)

    pl.semaphore_wait(barrier, count)

    mine = lax.div(z, 2)
    w_near = line(wsrc, weights.at[mine], w_sem, ((), ()), before,
                  jnp.logical_and(near_out, even))
    w_far = line(wsrc, weights.at[mine], w_sem, ((), ()), far_to, far_w_out)

    @chunks
    def _(c):
        w_near(c)
        w_far(c)

    def give(n):
        send_n[n] = block(owner((SUM_ODD[n], SUM_EVEN[n]), odd))
        push(send_n.at[n], got_n.at[n], n_sem, ((n,), (n,)), mate)

    def rotate():
        fetch[2].wait()
        fetch[3].wait()
        tokens = TOK // 2
        half = lax.broadcasted_iota(jnp.int32, (tokens, HEAD), 1) < HEAD // 2
        place = [
            jnp.broadcast_to(pos_ref[m : m + 1, :].astype(F32), (HEAD, HEAD)).T for m in range(2)
        ]
        index = lax.rem(lax.broadcasted_iota(jnp.int32, (1, HEAD), 1), HEAD // 2)
        freq = jnp.exp(index.astype(F32) * np.float32(-2.0 * np.log(500000.0) / HEAD))
        angle = jnp.where(half, place[0], place[1]) * freq
        here = (jnp.cos(angle), jnp.sin(angle))
        other = [pltpu.roll(v, HEAD // 2, 1) for v in here]
        for m in range(2):
            first, second = (here, other) if m == 0 else (other, here)
            cosine, sine = (jnp.where(half, a, b) for a, b in zip(first, second))
            sine = jnp.where(half, sine, -sine)
            span = pl.ds(m * tokens, tokens)
            for h in range(KW // HEAD):
                lanes = pl.ds(h * HEAD, HEAD)
                g = cot_ref[span, lanes].astype(F32)
                key[0, span, lanes] = (
                    g * cosine + pltpu.roll(g, HEAD // 2, 1) * sine
                ).astype(BF16)

        push(key.at[0], key.at[1], k_sem, ((0,), (0,)), mate)
        push(key.at[0], key_next.at[0], k_sem, ((1,), (1,)), before, s > 0)
        push(key.at[0], key_next.at[1], k_sem, ((2,), (2,)), far_before, far_out)

        @pl.when(s == LAST)
        def _():
            key_next[...] = jnp.zeros_like(key_next)

            @pl.when(even)
            def _():
                weights[mine] = wsrc[...]

    def own_weights():
        go = [
            line(weights.at[mine], weights.at[mine], g_sem, ((d, 0), (d, 0)), to[d], even)
            for d in range(2)
        ]

        @chunks
        def _(c):
            @pl.when(jnp.logical_and(s < LAST, even))
            def _():
                arrived(weights.at[mine, rows(c)], w_sem, (c,))

            for d in range(2):
                go[d](c)

    def key_forward():
        arrived(key.at[1], k_sem, (0,))
        push(key.at[1], key_next.at[1], k_sem, ((2,), (2,)), before, near_out)

    def term(n):
        arrived(got_n.at[n], n_sem, (n,))
        own = block(owner((SUM_EVEN[n], SUM_ODD[n]), odd))
        terms[n] = (
            jnp.dot(own, key[0], preferred_element_type=F32)
            + jnp.dot(got_n[n], key[1], preferred_element_type=F32)
        ).astype(BF16)

    def gather_step(j):
        spots, go = [], []
        for d in range(2):
            away = 2 * j + 2 - odd
            from_ = lax.rem(z + (2 * d - 1) * sign * away + 2 * RING, RING)
            spot = weights.at[lax.div(from_, 2)]
            slot = j + 1 - odd if j < 2 else 2
            spots.append(spot)
            if (j, d) != (2, 1):
                go.append(line(spot, spot, g_sem, ((d, slot), (d, slot)), to[d],
                               None if j < 2 else is_odd))

        @chunks
        def _(c):
            for d in range(2):
                def get():
                    arrived(spots[d].at[rows(c)], g_sem, (d, j, c))

                if (j, d) == (2, 1):
                    pl.when(is_odd)(get)
                else:
                    get()
                    go[d](c)

    def column(n):
        o = owner((GET_EVEN[n], GET_ODD[n]), odd)
        both = lax.dot_general(
            weights[lax.div(o, 2)], key_next[...].reshape(2 * TOK, KW),
            (((1,), (1,)), ((), ())), preferred_element_type=F32,
        )
        cols[pl.ds(pl.multiple_of(ROWS * o, 8), ROWS), :] = both[:ROWS, :TOK]
        send_c[n] = both[:, TOK:].astype(BF16)
        push(send_c.at[n], got_c.at[n], c_sem, ((n,), (n,)), mate)

    def sum_start():
        go = [
            line(terms.at[d], sums.at[d, 0], r_sem, ((d, 0), (d, 0)), to[d], when)
            for d, when in enumerate((even, is_odd))
        ]

        @chunks
        def _(c):
            for d in range(2):
                go[d](c)

    def sum_step(j):
        go, number = [], []
        for d in range(2):
            spot = sums.at[d, j]
            slot = j + 1 - odd if j < 2 else 2
            when = even if (d, j) == (1, 0) else None if j < 2 else is_odd
            go.append(line(spot, sums.at[d, slot], r_sem, ((d, slot), (d, slot)), to[d], when))
            number.append(2 * j + d + 1 - odd)
        if j == 2:
            pair = line(part, part, p_sem, ((), ()), mate, jnp.logical_and(outer, even))
            other = line(part, part_in, x_sem, ((), ()), across, jnp.logical_and(inner, even))

        @chunks
        def _(c):
            here = rows(c)
            for d in range(2):
                def add():
                    arrived(sums.at[d, j, here], r_sem, (d, j, c))
                    sums[d, j, here] = (
                        sums[d, j, here].astype(F32) + terms[number[d], here].astype(F32)
                    ).astype(BF16)

                if (d, j) == (1, 0):
                    pl.when(even)(add)
                elif j < 2:
                    add()
                else:
                    pl.when(is_odd)(add)
                go[d](c)
            if j == 2:

                @pl.when(even)
                def _():
                    for d in range(2):
                        arrived(sums.at[d, 2, here], r_sem, (d, 2, c))
                    part[here] = (
                        terms[5, here].astype(F32)
                        + sums[0, 2, here].astype(F32)
                        + sums[1, 2, here].astype(F32)
                    ).astype(BF16)

                pair(c)
                other(c)

    def keys_ready():
        @pl.when(s < LAST)
        def _():
            for m in range(2):
                arrived(key_next.at[m], k_sem, (1 + m,))

    def relay_step():
        relay = jnp.logical_and(inner, is_odd)
        go = line(part, part_in, x_sem, ((), ()), across, relay)

        @chunks
        def _(c):
            pl.when(relay)(lambda: arrived(part.at[rows(c)], p_sem, (c,)))
            go(c)

    def total_step():
        go = line(total_in, total_in, t_sem, ((), ()), mate, inner)

        @chunks
        def _(c):
            here = rows(c)

            @pl.when(inner)
            def _():
                arrived(part_in.at[here], x_sem, (c,))
                total_in[here] = (
                    part[here].astype(F32) + part_in[here].astype(F32)
                ).astype(BF16)

            go(c)

    def take(n):
        arrived(got_c.at[n], c_sem, (n,))
        o = owner((GET_ODD[n], GET_EVEN[n]), odd)
        cols[pl.ds(pl.multiple_of(ROWS * o, 8), ROWS), :] = got_c[n].astype(F32)[:ROWS]

    give(0)
    rotate()
    for n in range(1, 6):
        give(n)
    own_weights()
    gather_step(0)
    key_forward()
    gather_step(1)
    keys_ready()
    column(0)
    column(1)
    term(0)
    term(1)
    sum_start()
    column(2)
    column(3)
    gather_step(2)
    column(4)
    column(5)
    term(2)
    sum_step(0)
    term(3)
    term(4)
    sum_step(1)
    term(5)
    sum_step(2)
    relay_step()
    for n in range(4):
        take(n)
    total_step()
    take(4)
    take(5)

    for i in range(WIDTH // 512):
        out_ref[:, pl.ds(512 * i, 512)] = cols[pl.ds(512 * i, 512), :].T.astype(BF16)

    @chunks
    def _(c):
        pl.when(outer)(lambda: arrived(total_in.at[rows(c)], t_sem, (c,)))

    grad_ref[...] = total_in[...].astype(F32)[:ROWS].astype(BF16)

    for when, copy in pending:
        if when is None:
            copy.wait_send()
        else:
            pl.when(when)(copy.wait_send)

    @chunks
    def _(c):
        for finish in chunked:
            finish(c)


def per_device(normed, key_cotangent, positions, key_weight):
    vmem = pl.BlockSpec(memory_space=pltpu.VMEM)
    dma = pltpu.SemaphoreType.DMA
    grad, passed = pl.pallas_call(
        kernel,
        out_shape=(
            pltpu.VMEM((ROWS, KW), BF16),
            pltpu.VMEM((TOK, WIDTH), BF16),
        ),
        in_specs=[pl.BlockSpec(memory_space=pltpu.HBM)] * 4,
        out_specs=(vmem, vmem),
        scratch_shapes=[
            pltpu.VMEM((TOK, WIDTH), BF16),
            pltpu.VMEM((TOK, KW), BF16),
            pltpu.VMEM((2, TOK // 2), jnp.int32),
            pltpu.VMEM((ROWS, KW), BF16),
            pltpu.VMEM((RING * ROWS + 8, TOK), F32),
            pltpu.VMEM((6, PAD, TOK), BF16),
            pltpu.VMEM((6, PAD, TOK), BF16),
            pltpu.VMEM((2, TOK, KW), BF16),
            pltpu.VMEM((2, TOK, KW), BF16),
            pltpu.VMEM((PAD, KW), BF16),
            pltpu.VMEM((6, PAD, KW), BF16),
            pltpu.VMEM((6, PAD, KW), BF16),
            pltpu.VMEM((2, 3, PAD, KW), BF16),
            pltpu.VMEM((RING * ROWS, TOK), F32),
            pltpu.VMEM((6, PAD, TOK), BF16),
            pltpu.VMEM((6, PAD, TOK), BF16),
            pltpu.VMEM((PAD, KW), BF16),
            pltpu.VMEM((PAD, KW), BF16),
            pltpu.VMEM((PAD, KW), BF16),
            dma((4,)),
            dma((2, NC)),
            dma((2, 3)),
            dma((2, 6)),
            dma((2, 2, 3, NC)),
            dma((2, 2, 3, NC)),
            dma((2, 6)),
            dma((2, NC)),
            dma((2, NC)),
            dma((2, NC)),
        ],
        compiler_params=pltpu.CompilerParams(
            collective_id=0, has_side_effects=True, vmem_limit_bytes=52 << 20
        ),
        cost_estimate=pl.CostEstimate(
            flops=4 * TOK * KW * WIDTH, bytes_accessed=6 << 20, transcendentals=2 * TOK * HEAD
        ),
    )(
        normed.reshape(TOK, WIDTH),
        key_cotangent.reshape(TOK, KW),
        positions,
        key_weight.reshape(ROWS, KW),
    )
    return grad[None], passed.reshape(normed.shape)


def solution(mesh):
    in_specs = (
        P("section", None, ("shard", "replica"), None),
        P("section", None, ("shard", "replica"), None),
        P(None, ("shard", "replica")),
        P("section", "shard", None),
    )
    out_specs = (P("section", "shard", None), P("section", None, ("shard", "replica"), None))
    return jax.shard_map(
        per_device, mesh=mesh, in_specs=in_specs, out_specs=out_specs, check_vma=False
    )
```

time: 120 us -> 93.7 us (0.78)
  the two profiles are of different devices: /device:TPU:71 before, /device:TPU:1 now
where the time goes in v2:
time: 93.7 us; the launch traced here: 93.5 us
  Pallas kernels  90.8 us (97%)
  local copies, waits for them, and re-layouts  2.05 us (2%)
    pallas_call x1, Pallas kernels, per_device(): pl.pallas_call(kernel, out_shape=(pltpu.VMEM((ROWS, KW), BF16), pltpu.VME...  90.8 us
    unnamed x2, local copies, waits for them, and re-layouts  2.05 us

profile of v2, /device:TPU:1, one launch (start us, length us, event | category | flops | bytes accessed | tf_op | source)
XLA Modules:
  0.0 93.5 jit_solution(12050647210839909251)
XLA Ops:
  0.6 90.8 %shard_map.59 = (bf16[344,512]{1,0:T(8,128)(2,1)S(1)}, bf16[256,4096]{1,0:T(8,128)(2,1)S(1)}) custom-call(bf16[256,4096]{1,0:T(8,128)(2,1)} %bitcast.7, bf16[256,512]{1,0:T(8,128)(2,1)} %bitcast.9, s32[2,128]{1,0:T(2,128)} %pos_hbm.1, bf16[344,512]{1,0:T(8,128)(2,1)} %bitcast.8), custom_call_target="tpu_custom_call" | custom-call | flops 2147483648 | bytes 6291456 | tf_op jit(solution)/shard_map/pallas_call | solution.py:407
  91.5 0.7 copy.8
  92.2 1.3 %copy.9 = bf16[1,2,128,4096]{3,2,1,0:T(8,128)(2,1)} copy(bf16[1,2,128,4096]{3,2,1,0:T(8,128)(2,1)S(1)} %bitcast.5) | data formatting | bytes 4194304

commit v3 on v2

--- a/solution.py
+++ b/solution.py
@@ -17,7 +17,7 @@
 WIDTH = 4096
 LAST = 15
 FAR = 8
-CHUNKS = ((0, 96), (96, 96), (192, 80), (272, 80))
+CHUNKS = ((0, 64), (64, 64), (128, 64), (192, 64), (256, 48), (304, 48))
 NC = len(CHUNKS)
 MESH = pl.DeviceIdType.MESH
 SUM_EVEN, SUM_ODD = (6, 4, -4, 2, -2, 0), (5, -5, 3, -3, 1, -1)
@@ -30,7 +30,7 @@
     grad_ref, out_ref,
     normed, cot_ref, pos_ref, w_ref, flat, send_n, got_n, key, key_next, wsrc, weights, terms, sums,
     cols, send_c, got_c, part, part_in, total_in,
-    local_sem, w_sem, k_sem, n_sem, g_sem, r_sem, c_sem, p_sem, x_sem, t_sem,
+    local_sem, w_sem, k_sem, n_sem, g_sem, r_sem, c_sem, x_sem, t_sem,
 ):
     s, z, r = (lax.axis_index(a) for a in ("section", "shard", "replica"))
     inner = jnp.logical_or(r == 1, r == 2)
@@ -114,9 +114,9 @@
     for copy in fetch:
         copy.start()
     barrier = pltpu.get_barrier_semaphore()
-    count = jnp.int32(3)
+    count = jnp.int32(4)
     for when, device in (
-        (None, mate), (None, ahead), (None, behind), (inner, across),
+        (None, mate), (None, across), (None, ahead), (None, behind),
         (s > 0, before), (s < LAST, after), (far_out, far_before), (far_in, far_after),
         (far_w_out, far_to), (far_w_in, far_from),
     ):
@@ -134,6 +134,18 @@
         [w_ref[...].astype(F32), jnp.zeros((PAD - ROWS, KW), F32)], axis=0
     ).astype(BF16)
 
+    pl.semaphore_wait(barrier, count)
+
+    mine = lax.div(z, 2)
+    w_near = line(wsrc, weights.at[mine], w_sem, ((), ()), before,
+                  jnp.logical_and(near_out, even))
+    w_far = line(wsrc, weights.at[mine], w_sem, ((), ()), far_to, far_w_out)
+
+    @chunks
+    def _(c):
+        w_near(c)
+        w_far(c)
+
     fetch[1].wait()
     for i in range(WIDTH // 512):
         flat[pl.ds(512 * i, 512), :] = normed[:, pl.ds(512 * i, 512)].astype(F32).T
@@ -141,18 +153,6 @@
 
     def block(o):
         return flat[pl.ds(pl.multiple_of(ROWS * o, 8), PAD), :].astype(BF16)
-
-    pl.semaphore_wait(barrier, count)
-
-    mine = lax.div(z, 2)
-    w_near = line(wsrc, weights.at[mine], w_sem, ((), ()), before,
-                  jnp.logical_and(near_out, even))
-    w_far = line(wsrc, weights.at[mine], w_sem, ((), ()), far_to, far_w_out)
-
-    @chunks
-    def _(c):
-        w_near(c)
-        w_far(c)
 
     def give(n):
         send_n[n] = block(owner((SUM_ODD[n], SUM_EVEN[n]), odd))
@@ -276,8 +276,7 @@
             go.append(line(spot, sums.at[d, slot], r_sem, ((d, slot), (d, slot)), to[d], when))
             number.append(2 * j + d + 1 - odd)
         if j == 2:
-            pair = line(part, part, p_sem, ((), ()), mate, jnp.logical_and(outer, even))
-            other = line(part, part_in, x_sem, ((), ()), across, jnp.logical_and(inner, even))
+            other = line(part, part_in, x_sem, ((), ()), across, even)
 
         @chunks
         def _(c):
@@ -308,7 +307,6 @@
                         + sums[1, 2, here].astype(F32)
                     ).astype(BF16)
 
-                pair(c)
                 other(c)
 
     def keys_ready():
@@ -317,23 +315,14 @@
             for m in range(2):
                 arrived(key_next.at[m], k_sem, (1 + m,))
 
-    def relay_step():
-        relay = jnp.logical_and(inner, is_odd)
-        go = line(part, part_in, x_sem, ((), ()), across, relay)
-
-        @chunks
-        def _(c):
-            pl.when(relay)(lambda: arrived(part.at[rows(c)], p_sem, (c,)))
-            go(c)
-
     def total_step():
-        go = line(total_in, total_in, t_sem, ((), ()), mate, inner)
+        go = line(total_in, total_in, t_sem, ((), ()), mate, even)
 
         @chunks
         def _(c):
             here = rows(c)
 
-            @pl.when(inner)
+            @pl.when(even)
             def _():
                 arrived(part_in.at[here], x_sem, (c,))
                 total_in[here] = (
@@ -373,19 +362,16 @@
     sum_step(1)
     term(5)
     sum_step(2)
-    relay_step()
-    for n in range(4):
+    total_step()
+    for n in range(6):
         take(n)
-    total_step()
-    take(4)
-    take(5)
 
     for i in range(WIDTH // 512):
         out_ref[:, pl.ds(512 * i, 512)] = cols[pl.ds(512 * i, 512), :].T.astype(BF16)
 
     @chunks
     def _(c):
-        pl.when(outer)(lambda: arrived(total_in.at[rows(c)], t_sem, (c,)))
+        pl.when(is_odd)(lambda: arrived(total_in.at[rows(c)], t_sem, (c,)))
 
     grad_ref[...] = total_in[...].astype(F32)[:ROWS].astype(BF16)
 
@@ -441,7 +427,6 @@
             dma((2, 6)),
             dma((2, NC)),
             dma((2, NC)),
-            dma((2, NC)),
         ],
         compiler_params=pltpu.CompilerParams(
             collective_id=0, has_side_effects=True, vmem_limit_bytes=52 << 20

time: 93.7 us -> 94 us (level)
  the two profiles are of different devices: /device:TPU:1 before, /device:TPU:16 now
where the time goes in v3:
time: 94 us; the launch traced here: 93.9 us
  Pallas kernels  91.2 us (97%)
  local copies, waits for them, and re-layouts  2.05 us (2%)
    pallas_call x1, Pallas kernels, per_device(): pl.pallas_call(kernel, out_shape=(pltpu.VMEM((ROWS, KW), BF16), pltpu.VME...  91.2 us
    unnamed x2, local copies, waits for them, and re-layouts  2.05 us

profile of v3, /device:TPU:16, one launch (start us, length us, event | category | flops | bytes accessed | tf_op | source)
XLA Modules:
  0.0 93.9 jit_solution(12774987037034256456)
XLA Ops:
  0.6 91.2 %shard_map.59 = (bf16[344,512]{1,0:T(8,128)(2,1)S(1)}, bf16[256,4096]{1,0:T(8,128)(2,1)S(1)}) custom-call(bf16[256,4096]{1,0:T(8,128)(2,1)} %bitcast.7, bf16[256,512]{1,0:T(8,128)(2,1)} %bitcast.9, s32[2,128]{1,0:T(2,128)} %pos_hbm.1, bf16[344,512]{1,0:T(8,128)(2,1)} %bitcast.8), custom_call_target="tpu_custom_call" | custom-call | flops 2147483648 | bytes 6291456 | tf_op jit(solution)/shard_map/pallas_call | solution.py:393
  91.8 0.7 copy.8
  92.5 1.3 %copy.9 = bf16[1,2,128,4096]{3,2,1,0:T(8,128)(2,1)} copy(bf16[1,2,128,4096]{3,2,1,0:T(8,128)(2,1)S(1)} %bitcast.5) | data formatting | bytes 4194304

commit v4 on v2

--- a/solution.py
+++ b/solution.py
@@ -134,6 +134,18 @@
         [w_ref[...].astype(F32), jnp.zeros((PAD - ROWS, KW), F32)], axis=0
     ).astype(BF16)
 
+    pl.semaphore_wait(barrier, count)
+
+    mine = lax.div(z, 2)
+    w_near = line(wsrc, weights.at[mine], w_sem, ((), ()), before,
+                  jnp.logical_and(near_out, even))
+    w_far = line(wsrc, weights.at[mine], w_sem, ((), ()), far_to, far_w_out)
+
+    @chunks
+    def _(c):
+        w_near(c)
+        w_far(c)
+
     fetch[1].wait()
     for i in range(WIDTH // 512):
         flat[pl.ds(512 * i, 512), :] = normed[:, pl.ds(512 * i, 512)].astype(F32).T
@@ -141,18 +153,6 @@
 
     def block(o):
         return flat[pl.ds(pl.multiple_of(ROWS * o, 8), PAD), :].astype(BF16)
-
-    pl.semaphore_wait(barrier, count)
-
-    mine = lax.div(z, 2)
-    w_near = line(wsrc, weights.at[mine], w_sem, ((), ()), before,
-                  jnp.logical_and(near_out, even))
-    w_far = line(wsrc, weights.at[mine], w_sem, ((), ()), far_to, far_w_out)
-
-    @chunks
-    def _(c):
-        w_near(c)
-        w_far(c)
 
     def give(n):
         send_n[n] = block(owner((SUM_ODD[n], SUM_EVEN[n]), odd))
@@ -355,12 +355,12 @@
     gather_step(0)
     key_forward()
     gather_step(1)
+    term(0)
+    term(1)
+    sum_start()
     keys_ready()
     column(0)
     column(1)
-    term(0)
-    term(1)
-    sum_start()
     column(2)
     column(3)
     gather_step(2)

time: 93.7 us -> 94.3 us (level)
  no operation moved by 1% of the time
where the time goes in v4:
time: 94.3 us; the launch traced here: 94.2 us
  Pallas kernels  91.5 us (97%)
  local copies, waits for them, and re-layouts  2.05 us (2%)
    pallas_call x1, Pallas kernels, per_device(): pl.pallas_call(kernel, out_shape=(pltpu.VMEM((ROWS, KW), BF16), pltpu.VME...  91.5 us
    unnamed x2, local copies, waits for them, and re-layouts  2.05 us

profile of v4, /device:TPU:1, one launch (start us, length us, event | category | flops | bytes accessed | tf_op | source)
XLA Modules:
  0.0 94.2 jit_solution(16042791636096342110)
XLA Ops:
  0.6 91.5 %shard_map.59 = (bf16[344,512]{1,0:T(8,128)(2,1)S(1)}, bf16[256,4096]{1,0:T(8,128)(2,1)S(1)}) custom-call(bf16[256,4096]{1,0:T(8,128)(2,1)} %bitcast.7, bf16[256,512]{1,0:T(8,128)(2,1)} %bitcast.9, s32[2,128]{1,0:T(2,128)} %pos_hbm.1, bf16[344,512]{1,0:T(8,128)(2,1)} %bitcast.8), custom_call_target="tpu_custom_call" | custom-call | flops 2147483648 | bytes 6291456 | tf_op jit(solution)/shard_map/pallas_call | solution.py:407
  92.1 0.7 copy.8
  92.8 1.3 %copy.9 = bf16[1,2,128,4096]{3,2,1,0:T(8,128)(2,1)} copy(bf16[1,2,128,4096]{3,2,1,0:T(8,128)(2,1)S(1)} %bitcast.5) | data formatting | bytes 4194304
